TPU v7x, 256 devices: a whole 4x4x8 slice. The times are simulated.
256 devices in a mesh: pool: 2 (over y_hi), fsdp: 64 (over z, y_lo, x), rep: 2 (over core).
Axes of the slice: x: 4, y: 4 (y_hi: 2, y_lo: 2; y = y_hi * 2 + y_lo), z: 8, core: 2. Of those that a mesh axis runs over, the one named last changes fastest.
Arguments:
- master: float32 [6144, 16384], P(('pool', 'fsdp', 'rep')), may hold values from -6 to 6
- grad: bfloat16 [6144, 16384], P(('pool', 'fsdp', 'rep')), may hold values from -6 to 6
- first_moment: float32 [6144, 16384], P(('pool', 'fsdp', 'rep')), may hold values from -6 to 6
- second_moment: float32 [6144, 16384], P(('pool', 'fsdp', 'rep')), may hold values from 0.05 to 2
- matching: int32 [64], replicated, may hold values from 0 to 63, each once
Outputs:
- new_master: float32 [6144, 16384], P(('pool', 'fsdp', 'rep'))
- new_first: float32 [6144, 16384], P(('pool', 'fsdp', 'rep'))
- new_second: float32 [6144, 16384], P(('pool', 'fsdp', 'rep'))
- rollout_weight: bfloat16 [64, 6144, 256], P('fsdp')
Inputs may be any that keep to these rules, and one draw needn't show every extreme that they name: matching is a permutation: rollout rank r is hosted at fsdp index matching[r].
All inputs are finite; a program needn't handle non-finite values.
Results may differ from a plain program's by a relative error of at most 0.001.
Values may be sent and summed in bfloat16 or wider, within the bound.
A program may use at most 64 MiB of HBM per device.

v0:
```python
import jax
import jax.numpy as jnp
from jax import lax
from jax.sharding import PartitionSpec as P

beta_one = 0.9
beta_two = 0.95
learn_rate = 0.05
decay_rate = 0.1
epsilon = 1e-08
bias_one = 1.0 - 0.9**10
bias_two = 1.0 - 0.95**10


def adamw_step(master, grad, first_moment, second_moment):
    gradient = grad.astype(jnp.float32)
    new_first = beta_one * first_moment + (1.0 - beta_one) * gradient
    new_second = beta_two * second_moment + (1.0 - beta_two) * gradient * gradient
    update = new_first / bias_one / (jnp.sqrt(new_second / bias_two) + epsilon)
    new_master = master * (1.0 - learn_rate * decay_rate) - learn_rate * update
    return (new_master, new_first, new_second)


def per_device(master, grad, first_moment, second_moment, matching):
    new_master, new_first, new_second = adamw_step(master, grad, first_moment, second_moment)
    weights = new_master.astype(jnp.bfloat16)
    count = matching.shape[0]
    inverse = jnp.zeros_like(matching).at[matching].set(lax.iota(jnp.int32, count))
    rows, width = weights.shape
    cols = width // count
    pieces = jnp.take(weights.reshape(rows, count, cols), inverse, axis=1)
    arrived = lax.all_to_all(pieces, "fsdp", split_axis=1, concat_axis=0, tiled=True)
    crossed = lax.all_gather(arrived.reshape(1, count, 1, rows, cols), "pool", axis=0, tiled=True)
    whole = lax.all_gather(crossed, "rep", axis=2, tiled=True)
    rollout_weight = whole.reshape(1, -1, cols)
    return (new_master, new_first, new_second, rollout_weight)


def solution(mesh):
    return jax.shard_map(
        per_device,
        mesh=mesh,
        in_specs=(
            P(("pool", "fsdp", "rep"), None),
            P(("pool", "fsdp", "rep"), None),
            P(("pool", "fsdp", "rep"), None),
            P(("pool", "fsdp", "rep"), None),
            P(),
        ),
        out_specs=(
            P(("pool", "fsdp", "rep"), None),
            P(("pool", "fsdp", "rep"), None),
            P(("pool", "fsdp", "rep"), None),
            P("fsdp", None, None),
        ),
        check_vma=False,
    )
```

profile of v0, /device:TPU:65, one launch (start us, length us, event | category | flops | bytes accessed | tf_op | source)
XLA Modules:
  0.0 110.9 jit_solution(10621033522853543395)
XLA Ops:
  7.2 0.0 all-gather.6.cloned.1.call-start
  7.2 0.7 compare_select_fusion.1
  7.9 0.8 scatter_custom_fusion
  8.7 5.5 %fusion.4 = (bf16[24,16384]{1,0:T(8,128)(2,1)S(1)}, f32[24,16384]{1,0:T(8,128)}, f32[24,16384]{1,0:T(8,128)}, f32[24,16384]{1,0:T(8,128)}) fusion(f32[24,16384]{1,0:T(8,128)} %param.5, bf16[24,16384]{1,0:T(8,128)(2,1)} %param.6, f32[24,16384]{1,0:T(8,128)} %param.7, f32[24,16384]{1,0:T(8,128)} %param.8), kind=kLoop, calls=%fused_computation.15 | loop fusion | flops 6291456 | bytes 11010048 | tf_op jit(solution)/shard_map/convert_element_type | solution.py:26
  14.2 0.1 copy.20
  14.3 0.6 gather_fusion
  14.9 0.1 select_bitcast_fusion
  15.0 30.7 %all_to_all.15 = bf16[24,64,256]{2,0,1:T(8,128)(2,1)} all-to-all(bf16[24,64,256]{2,0,1:T(8,128)(2,1)S(1)} %select_bitcast_fusion), channel_id=1, replica_groups=mesh['pool'=2,'fsdp'=64,'rep'=2] {'fsdp'}, dimensions={1} | all-to-all | bytes 1572864 | tf_op jit(solution)/shard_map/all_to_all | solution.py:32
  45.7 0.0 all-gather.6.cloned.1.call-update
  45.8 0.0 all-gather.4.cloned.1.call-start
  45.8 35.2 %all-gather.6.cloned.1.call-done = bf16[128,24,1,256]{3,1,2,0:T(8,128)(2,1)} async-done(((bf16[64,24,1,256]{3,1,2,0:T(8,128)(2,1)}), bf16[128,24,1,256]{3,1,2,0:T(8,128)(2,1)}) %all-gather.6.cloned.1.call-update) | async-done | bytes 1572880 | tf_op jit(solution)/shard_map/all_gather | solution.py:33
  81.0 0.0 all-gather.4.cloned.1.call-update
  81.1 19.2 %all-gather.4.cloned.1.call-done = bf16[2,64,2,24,256]{4,3,1,0,2:T(8,128)(2,1)} async-done(((bf16[2,64,1,24,256]{4,3,1,0,2:T(8,128)(2,1)}), bf16[2,64,2,24,256]{4,3,1,0,2:T(8,128)(2,1)}) %all-gather.4.cloned.1.call-update) | async-done | bytes 3145744 | tf_op jit(solution)/shard_map/all_gather | solution.py:34
  100.2 3.8 %copy.17 = bf16[2,64,2,24,256]{4,3,2,1,0:T(8,128)(2,1)} copy(bf16[2,64,2,24,256]{4,3,1,0,2:T(8,128)(2,1)} %all-gather.4.cloned.1.call-done) | data formatting | bytes 6291456 | tf_op jit(solution)/shard_map/all_gather | solution.py:34
  (4 shorter events, 0.0 us)
Async XLA Ops:
  7.2 73.9 %all-gather.6.cloned.1.call-start = ((), (), s32[]{:S(2)}) async-start(), calls=%async_computation.2 | async-start | bytes 2359296 | tf_op jit(solution)/shard_map/all_gather | solution.py:33
  45.8 54.5 %all-gather.4.cloned.1.call-start = ((), (), s32[]{:S(2)}) async-start(), calls=%async_computation.1 | async-start | bytes 4718592 | tf_op jit(solution)/shard_map/all_gather | solution.py:34
Sparse Core Ops, SparseCore 0:
  45.9 35.1 all-gather.5
  82.8 17.3 all-gather.3
where the time goes:
time: 113 us; the launch traced here: 111 us
  waiting for transfers between devices  54.4 us (48%)
  blocking collectives  30.7 us (27%)
  between operations  14.1 us (12%)
  other arithmetic  6.34 us (6%)
  local copies, waits for them, and re-layouts  5.23 us (5%)
    all_gather x1, waiting for transfers between devices, per_device(): lax.all_gather(arrived.reshape(1, count, 1, rows, cols), 'pool', axis=0,...  35.2 us
    all_to_all x1, blocking collectives, per_device(): lax.all_to_all(pieces, 'fsdp', split_axis=1, concat_axis=0, tiled=True)  30.7 us
    all_gather x1, waiting for transfers between devices, per_device(): whole = lax.all_gather(crossed, 'rep', axis=2, tiled=True)  19.2 us
    convert_element_type x1, other arithmetic, per_device(): weights = new_master.astype(jnp.bfloat16)  5.52 us
    all_gather x1, local copies, waits for them, and re-layouts, per_device(): whole = lax.all_gather(crossed, 'rep', axis=2, tiled=True)  3.8 us
  transfers between devices with their start and end apart: 2, of which 2 were waited for; matrix products, arithmetic and copies ran while one was open for 0% of the time, Pallas kernels for 0%

commit v1 on v0

v1 whole, which is shorter than its diff:
```python
import functools

import jax
import jax.numpy as jnp
from jax import lax
from jax.experimental import pallas as pl
from jax.experimental.pallas import tpu as pltpu
from jax.sharding import PartitionSpec as P

MESH = pl.DeviceIdType.MESH
beta_one = 0.9
beta_two = 0.95
learn_rate = 0.05
decay_rate = 0.1
epsilon = 1e-08
bias_one = 1.0 - 0.9**10
bias_two = 1.0 - 0.95**10

NX, NY, NZ = 4, 4, 8
STEPS = NX * NZ
GROUP = NX
GROUPS = STEPS // GROUP
CHUNKS = 8
LAG = 3


def place():
    pool, fsdp, core = lax.axis_index("pool"), lax.axis_index("fsdp"), lax.axis_index("rep")
    return fsdp % NX, pool * 2 + (fsdp // NX) % 2, fsdp // (2 * NX), core


def device(x, y, z, core):
    x, y, z, core = (x + NX) % NX, (y + NY) % NY, (z + NZ) % NZ, core % 2
    return (y // 2, z * (2 * NX) + (y % 2) * NX + x, core)


def offset(k):
    j = k // NX
    return k % NX, ((j + 1) // 2) * (2 * (j % 2) - 1)


def adamw(master, grad, first, second):
    gradient = grad.astype(jnp.float32)
    new_first = beta_one * first + (1.0 - beta_one) * gradient
    new_second = beta_two * second + (1.0 - beta_two) * gradient * gradient
    step = new_first * (learn_rate / bias_one)
    new_master = master * (1.0 - learn_rate * decay_rate) - step / (jnp.sqrt(new_second * (1.0 / bias_two)) + epsilon)
    return new_master, new_first, new_second


def kernel(
    master_hbm, grad_hbm, first_hbm, second_hbm, matching_ref,
    new_master, new_first, new_second, rollout,
    master, grad, first, second, weights, row, ranks, packed, held,
    in_sem, rank_sem, plane_send, plane_recv, y_send, y_recv, core_send, core_recv,
):
    rows, width = master.shape
    count = matching_ref.shape[1]
    cols = width // count
    half = cols // 2
    x, y, z, core = place()
    other = device(x, y, z, core + 1)

    grad_load = pltpu.make_async_copy(grad_hbm, grad, in_sem.at[0, 0])
    grad_load.start()

    def load(t, i):
        where = pl.ds(t * (width // CHUNKS), width // CHUNKS)
        src, dst = ((master_hbm, master), (first_hbm, first), (second_hbm, second))[i]
        return pltpu.make_async_copy(src.at[:, where], dst.at[:, where], in_sem.at[1 + i, t])

    for t in range(CHUNKS):
        for i in range(3):
            load(t, i).start()

    barrier = pltpu.get_barrier_semaphore()

    def greet(k, carry):
        dx, dz = offset(k)
        pl.semaphore_signal(barrier, inc=1, device_id=device(x + dx, y, z + dz, core), device_id_type=MESH)
        return carry

    lax.fori_loop(1, STEPS, greet, 0)
    for dy in (1, 2, 3):
        pl.semaphore_signal(barrier, inc=1, device_id=device(x, y + dy, z, core), device_id_type=MESH)
    pl.semaphore_signal(barrier, inc=1, device_id=other, device_id_type=MESH)

    lane = lax.broadcasted_iota(jnp.int32, (count, count), 1)
    sub = lax.broadcasted_iota(jnp.int32, (count, count), 0)
    hit = jnp.where(matching_ref[...] == sub, lane, 0)
    column = jnp.max(hit, axis=1, keepdims=True)
    row[...] = jnp.sum(jnp.where(lane == sub, column, 0), axis=0, keepdims=True)
    to_scalar = pltpu.make_async_copy(row, ranks, rank_sem)
    to_scalar.start()
    to_scalar.wait()
    grad_load.wait()
    for t in range(CHUNKS):
        for i in range(3):
            load(t, i).wait()

        def block(n, carry):
            where = pl.ds(pl.multiple_of(n * cols, cols), cols)
            value, new_first[:, where], new_second[:, where] = adamw(
                master[:, where], grad[:, where], first[:, where], second[:, where]
            )
            new_master[:, where] = value
            weights[n] = jnp.concatenate([value[:, :half], value[:, half:]], axis=0).astype(jnp.bfloat16)
            return carry

        lax.fori_loop(t * (count // CHUNKS), (t + 1) * (count // CHUNKS), block, 0)

    def piece(dx, dz, parity):
        host = ((z + NZ + dz) % NZ) * (2 * NX) + ((y + parity) % 2) * NX + (x + dx) % NX
        return weights[ranks[0, host]]

    held[core, 0, 0] = piece(0, 0, 1)
    held[core, 1, 0] = piece(0, 0, 0)
    pl.semaphore_wait(barrier, STEPS - 1 + 3 + 1)

    def send(k, carry):
        dx, dz = offset(k)
        packed[k, 0] = piece(dx, dz, 1)
        packed[k, 1] = piece(dx, dz, 0)
        pltpu.make_async_remote_copy(
            src_ref=packed.at[k],
            dst_ref=held.at[core, pl.ds(0, 2), k],
            send_sem=plane_send,
            recv_sem=plane_recv.at[k // GROUP],
            device_id=device(x + dx, y, z + dz, core),
            device_id_type=MESH,
        ).start()
        return carry

    lax.fori_loop(1, STEPS, send, 0)

    def arrived(g):
        low = max(g * GROUP, 1)
        where = held.at[core, pl.ds(0, 2), pl.ds(low, (g + 1) * GROUP - low)]
        return pltpu.make_async_remote_copy(
            src_ref=where, dst_ref=where, send_sem=plane_send, recv_sem=plane_recv.at[g], device_id=other, device_id_type=MESH
        )

    def over_y(g, dy):
        here = pl.ds(g * GROUP, GROUP)
        return pltpu.make_async_remote_copy(
            src_ref=held.at[core, 1 if dy == 2 else 0, here],
            dst_ref=held.at[core, 1 + dy, here],
            send_sem=y_send.at[dy - 1],
            recv_sem=y_recv.at[dy - 1, g],
            device_id=device(x, y + dy, z, core),
            device_id_type=MESH,
        )

    def over_chip(g):
        where = held.at[core, pl.ds(1, 4), pl.ds(g * GROUP, GROUP)]
        return pltpu.make_async_remote_copy(
            src_ref=where, dst_ref=where, send_sem=core_send, recv_sem=core_recv.at[g], device_id=other, device_id_type=MESH
        )

    def assemble(g):
        def block(n, carry):
            i, k = n // GROUP, g * GROUP + n % GROUP
            dx, dz = offset(k)
            pool, fsdp, _ = device(x + NX - dx, y + NY - i, z + NZ - dz, 0)
            start = pl.multiple_of((pool * count + fsdp) * (2 * rows), 2 * rows)
            parts = []
            for c in (0, 1):
                value = held[c, 1 + i, k].astype(jnp.float32)
                parts.append(jnp.concatenate([value[:rows], value[rows:]], axis=1))
            rollout[pl.ds(start, 2 * rows), :] = jnp.concatenate(parts, axis=0).astype(jnp.bfloat16)
            return carry

        lax.fori_loop(0, 4 * GROUP, block, 0)

    for t in range(GROUPS + LAG + 1):
        if t < GROUPS:
            arrived(t).wait_recv()
            for dy in (1, 2, 3):
                over_y(t, dy).start()
        if 0 <= t - LAG < GROUPS:
            for dy in (1, 2, 3):
                over_y(t - LAG, dy).wait_recv()
            over_chip(t - LAG).start()
        if 0 <= t - LAG - 1 < GROUPS:
            over_chip(t - LAG - 1).wait_recv()
            assemble(t - LAG - 1)

    def drain(ref, sem):
        pltpu.make_async_remote_copy(
            src_ref=ref, dst_ref=ref, send_sem=sem, recv_sem=plane_recv.at[0], device_id=other, device_id_type=MESH
        ).wait_send()

    drain(packed.at[pl.ds(1, STEPS - 1)], plane_send)
    for dy in (1, 2, 3):
        drain(held.at[core, 1 if dy == 2 else 0], y_send.at[dy - 1])
    drain(held.at[core, pl.ds(1, 4)], core_send)


def per_device(master, grad, first_moment, second_moment, matching):
    rows, width = master.shape
    count = matching.shape[0]
    cols = width // count
    total = 2 * count * 2 * rows
    hbm = pl.BlockSpec(memory_space=pltpu.HBM)
    vmem = pl.BlockSpec(memory_space=pltpu.VMEM)
    dma = pltpu.SemaphoreType.DMA
    new_master, new_first, new_second, rollout = pl.pallas_call(
        kernel,
        out_shape=[pltpu.VMEM((rows, width), jnp.float32)] * 3 + [pltpu.VMEM((total, cols), jnp.bfloat16)],
        in_specs=[hbm] * 4 + [vmem],
        out_specs=[vmem] * 4,
        scratch_shapes=[
            pltpu.VMEM((rows, width), jnp.float32),
            pltpu.VMEM((rows, width), jnp.bfloat16),
            pltpu.VMEM((rows, width), jnp.float32),
            pltpu.VMEM((rows, width), jnp.float32),
            pltpu.VMEM((count, 2 * rows, cols // 2), jnp.bfloat16),
            pltpu.VMEM((1, count), jnp.int32),
            pltpu.SMEM((1, count), jnp.int32),
            pltpu.VMEM((STEPS, 2, 2 * rows, cols // 2), jnp.bfloat16),
            pltpu.VMEM((2, 5, STEPS, 2 * rows, cols // 2), jnp.bfloat16),
            dma((4, CHUNKS)),
            dma,
            dma,
            dma((GROUPS,)),
            dma((3,)),
            dma((3, GROUPS)),
            dma,
            dma((GROUPS,)),
        ],
        compiler_params=pltpu.CompilerParams(collective_id=0, has_side_effects=True, vmem_limit_bytes=30 << 20),
    )(master, grad, first_moment, second_moment, matching.reshape(1, count))
    return new_master, new_first, new_second, rollout.reshape(1, total, cols)


def solution(mesh):
    rows = P(("pool", "fsdp", "rep"), None)
    return jax.shard_map(
        per_device,
        mesh=mesh,
        in_specs=(rows, rows, rows, rows, P()),
        out_specs=(rows, rows, rows, P("fsdp", None, None)),
        check_vma=False,
    )
```

time: 113 us -> 53.8 us (0.48)
  the two profiles are of different devices: /device:TPU:65 before, /device:TPU:1 now
where the time goes in v1:
time: 53.8 us; the launch traced here: 53.6 us
  Pallas kernels  41.9 us (78%)
  local copies, waits for them, and re-layouts  11.1 us (21%)
  between operations  0.65 us (1%)
    pallas_call x1, Pallas kernels, per_device(): pl.pallas_call(kernel, out_shape=[pltpu.VMEM((rows, width), jnp.float32)]...  41.9 us
    unnamed x14, local copies, waits for them, and re-layouts  11.1 us

profile of v1, /device:TPU:1, one launch (start us, length us, event | category | flops | bytes accessed | tf_op | source)
XLA Modules:
  0.0 53.6 jit_solution(5813947854717935945)
XLA Ops:
  0.6 0.0 copy-start
  0.6 1.4 %copy-done = f32[24,16384]{1,0:T(8,128)S(1)} copy-done((f32[24,16384]{1,0:T(8,128)S(1)}, f32[24,16384]{1,0:T(8,128)}, u32[]{:S(2)}) %copy-start) | copy-done | bytes 1572888
  2.0 0.0 copy-start.1
  2.0 1.4 %copy-done.1 = f32[24,16384]{1,0:T(8,128)S(1)} copy-done((f32[24,16384]{1,0:T(8,128)S(1)}, f32[24,16384]{1,0:T(8,128)}, u32[]{:S(2)}) %copy-start.1) | copy-done | bytes 1572888
  3.4 0.0 copy-start.2
  3.5 1.4 %copy-done.2 = f32[24,16384]{1,0:T(8,128)S(1)} copy-done((f32[24,16384]{1,0:T(8,128)S(1)}, f32[24,16384]{1,0:T(8,128)}, u32[]{:S(2)}) %copy-start.2) | copy-done | bytes 1572888
  4.9 0.0 copy-start.3
  4.9 1.1 %copy-done.3 = bf16[24,16384]{1,0:T(8,128)(2,1)S(1)} copy-done((bf16[24,16384]{1,0:T(8,128)(2,1)S(1)}, bf16[24,16384]{1,0:T(8,128)(2,1)}, u32[]{:S(2)}) %copy-start.3) | copy-done | bytes 786456
  6.0 0.0 copy-start.4
  6.0 0.7 %copy-done.4 = s32[64]{0:T(128)S(1)} copy-done((s32[64]{0:T(128)S(1)}, s32[64]{0:T(128)}, u32[]{:S(2)}) %copy-start.4) | copy-done | bytes 280
  6.6 41.9 %shard_map.84 = (f32[24,16384]{1,0:T(8,128)S(1)}, f32[24,16384]{1,0:T(8,128)S(1)}, f32[24,16384]{1,0:T(8,128)S(1)}, bf16[6144,256]{1,0:T(8,128)(2,1)S(1)}) custom-call(f32[24,16384]{1,0:T(8,128)S(1)} %copy-done, bf16[24,16384]{1,0:T(8,128)(2,1)S(1)} %copy-done.3, f32[24,16384]{1,0:T(8,128)S(1)} %copy-done.1, f32[24,16384]{1,0:T(8,128)S(1)} %copy-done.2, ...), custom_call_target="tpu_custom_call" | custom-call | tf_op jit(solution)/shard_map/pallas_call | solution.py:207
  48.5 1.1 %copy.13 = f32[24,16384]{1,0:T(8,128)} copy(f32[24,16384]{1,0:T(8,128)S(1)} %get-tuple-element.12) | data formatting | bytes 3145728
  49.7 1.1 %copy.14 = f32[24,16384]{1,0:T(8,128)} copy(f32[24,16384]{1,0:T(8,128)S(1)} %get-tuple-element.13) | data formatting | bytes 3145728
  50.8 1.1 %copy.15 = f32[24,16384]{1,0:T(8,128)} copy(f32[24,16384]{1,0:T(8,128)S(1)} %get-tuple-element.14) | data formatting | bytes 3145728
  52.0 1.7 %copy.16 = bf16[1,6144,256]{2,1,0:T(8,128)(2,1)} copy(bf16[1,6144,256]{2,1,0:T(8,128)(2,1)S(1)} %bitcast.2) | data formatting | bytes 6291456
Async XLA Ops:
  0.6 1.4 %copy-start = (f32[24,16384]{1,0:T(8,128)S(1)}, f32[24,16384]{1,0:T(8,128)}, u32[]{:S(2)}) copy-start(f32[24,16384]{1,0:T(8,128)} %master_hbm.1) | copy-start | bytes 4718596
  2.0 1.4 %copy-start.1 = (f32[24,16384]{1,0:T(8,128)S(1)}, f32[24,16384]{1,0:T(8,128)}, u32[]{:S(2)}) copy-start(f32[24,16384]{1,0:T(8,128)} %first_hbm.1) | copy-start | bytes 4718596
  3.4 1.4 %copy-start.2 = (f32[24,16384]{1,0:T(8,128)S(1)}, f32[24,16384]{1,0:T(8,128)}, u32[]{:S(2)}) copy-start(f32[24,16384]{1,0:T(8,128)} %second_hbm.1) | copy-start | bytes 4718596
  4.9 1.1 %copy-start.3 = (bf16[24,16384]{1,0:T(8,128)(2,1)S(1)}, bf16[24,16384]{1,0:T(8,128)(2,1)}, u32[]{:S(2)}) copy-start(bf16[24,16384]{1,0:T(8,128)(2,1)} %grad_hbm.1) | copy-start | bytes 2359300
  6.0 0.7 %copy-start.4 = (s32[64]{0:T(128)S(1)}, s32[64]{0:T(128)}, u32[]{:S(2)}) copy-start(s32[64]{0:T(128)} %param.9) | copy-start | bytes 772

commit v2 on v1

--- a/solution.py
+++ b/solution.py
@@ -18,10 +18,13 @@
 
 NX, NY, NZ = 4, 4, 8
 STEPS = NX * NZ
-GROUP = NX
-GROUPS = STEPS // GROUP
+GROUPS = (
+    (0, 4, 3.0), (4, 4, 6.0), (8, 4, 6.2), (12, 4, 10.0), (16, 4, 10.2),
+    (20, 2, 12.5), (24, 2, 12.7), (22, 2, 15.0), (26, 2, 15.2),
+    (28, 1, 15.6), (29, 1, 17.0), (30, 1, 18.5), (31, 1, 19.5),
+)
+Y_TIME, CHIP_TIME = 3.5, 1.5
 CHUNKS = 8
-LAG = 3
 
 
 def place():
@@ -49,18 +52,20 @@
 
 
 def kernel(
-    master_hbm, grad_hbm, first_hbm, second_hbm, matching_ref,
+    master_hbm, grad_hbm, first_hbm, second_hbm, matching_hbm,
     new_master, new_first, new_second, rollout,
-    master, grad, first, second, weights, row, ranks, packed, held,
+    master, grad, first, second, weights, matching, row, ranks, packed, held,
     in_sem, rank_sem, plane_send, plane_recv, y_send, y_recv, core_send, core_recv,
 ):
     rows, width = master.shape
-    count = matching_ref.shape[1]
+    count = matching_hbm.shape[1]
     cols = width // count
     half = cols // 2
     x, y, z, core = place()
     other = device(x, y, z, core + 1)
 
+    matching_load = pltpu.make_async_copy(matching_hbm, matching, rank_sem)
+    matching_load.start()
     grad_load = pltpu.make_async_copy(grad_hbm, grad, in_sem.at[0, 0])
     grad_load.start()
 
@@ -85,9 +90,10 @@
         pl.semaphore_signal(barrier, inc=1, device_id=device(x, y + dy, z, core), device_id_type=MESH)
     pl.semaphore_signal(barrier, inc=1, device_id=other, device_id_type=MESH)
 
+    matching_load.wait()
     lane = lax.broadcasted_iota(jnp.int32, (count, count), 1)
     sub = lax.broadcasted_iota(jnp.int32, (count, count), 0)
-    hit = jnp.where(matching_ref[...] == sub, lane, 0)
+    hit = jnp.where(matching[...] == sub, lane, 0)
     column = jnp.max(hit, axis=1, keepdims=True)
     row[...] = jnp.sum(jnp.where(lane == sub, column, 0), axis=0, keepdims=True)
     to_scalar = pltpu.make_async_copy(row, ranks, rank_sem)
@@ -117,31 +123,36 @@
     held[core, 1, 0] = piece(0, 0, 0)
     pl.semaphore_wait(barrier, STEPS - 1 + 3 + 1)
 
-    def send(k, carry):
-        dx, dz = offset(k)
-        packed[k, 0] = piece(dx, dz, 1)
-        packed[k, 1] = piece(dx, dz, 0)
-        pltpu.make_async_remote_copy(
-            src_ref=packed.at[k],
-            dst_ref=held.at[core, pl.ds(0, 2), k],
-            send_sem=plane_send,
-            recv_sem=plane_recv.at[k // GROUP],
-            device_id=device(x + dx, y, z + dz, core),
-            device_id_type=MESH,
-        ).start()
-        return carry
-
-    lax.fori_loop(1, STEPS, send, 0)
+    def sender(g):
+        def send(k, carry):
+            dx, dz = offset(k)
+            packed[k, 0] = piece(dx, dz, 1)
+            packed[k, 1] = piece(dx, dz, 0)
+            pltpu.make_async_remote_copy(
+                src_ref=packed.at[k],
+                dst_ref=held.at[core, pl.ds(0, 2), k],
+                send_sem=plane_send,
+                recv_sem=plane_recv.at[g],
+                device_id=device(x + dx, y, z + dz, core),
+                device_id_type=MESH,
+            ).start()
+            return carry
+
+        return send
+
+    for g, (low, size, _) in sorted(enumerate(GROUPS), key=lambda item: item[1][0]):
+        lax.fori_loop(max(low, 1), low + size, sender(g), 0)
 
     def arrived(g):
-        low = max(g * GROUP, 1)
-        where = held.at[core, pl.ds(0, 2), pl.ds(low, (g + 1) * GROUP - low)]
+        low, size, _ = GROUPS[g]
+        low, size = max(low, 1), low + size - max(low, 1)
+        where = held.at[core, pl.ds(0, 2), pl.ds(low, size)]
         return pltpu.make_async_remote_copy(
             src_ref=where, dst_ref=where, send_sem=plane_send, recv_sem=plane_recv.at[g], device_id=other, device_id_type=MESH
         )
 
     def over_y(g, dy):
-        here = pl.ds(g * GROUP, GROUP)
+        here = pl.ds(*GROUPS[g][:2])
         return pltpu.make_async_remote_copy(
             src_ref=held.at[core, 1 if dy == 2 else 0, here],
             dst_ref=held.at[core, 1 + dy, here],
@@ -152,14 +163,16 @@
         )
 
     def over_chip(g):
-        where = held.at[core, pl.ds(1, 4), pl.ds(g * GROUP, GROUP)]
+        where = held.at[core, pl.ds(1, 4), pl.ds(*GROUPS[g][:2])]
         return pltpu.make_async_remote_copy(
             src_ref=where, dst_ref=where, send_sem=core_send, recv_sem=core_recv.at[g], device_id=other, device_id_type=MESH
         )
 
     def assemble(g):
+        low, size, _ = GROUPS[g]
+
         def block(n, carry):
-            i, k = n // GROUP, g * GROUP + n % GROUP
+            i, k = n // size, low + n % size
             dx, dz = offset(k)
             pool, fsdp, _ = device(x + NX - dx, y + NY - i, z + NZ - dz, 0)
             start = pl.multiple_of((pool * count + fsdp) * (2 * rows), 2 * rows)
@@ -170,20 +183,27 @@
             rollout[pl.ds(start, 2 * rows), :] = jnp.concatenate(parts, axis=0).astype(jnp.bfloat16)
             return carry
 
-        lax.fori_loop(0, 4 * GROUP, block, 0)
-
-    for t in range(GROUPS + LAG + 1):
-        if t < GROUPS:
-            arrived(t).wait_recv()
-            for dy in (1, 2, 3):
-                over_y(t, dy).start()
-        if 0 <= t - LAG < GROUPS:
-            for dy in (1, 2, 3):
-                over_y(t - LAG, dy).wait_recv()
-            over_chip(t - LAG).start()
-        if 0 <= t - LAG - 1 < GROUPS:
-            over_chip(t - LAG - 1).wait_recv()
-            assemble(t - LAG - 1)
+        lax.fori_loop(0, 4 * size, block, 0)
+
+    def take_plane(g):
+        arrived(g).wait_recv()
+        for dy in (1, 2, 3):
+            over_y(g, dy).start()
+
+    def take_y(g):
+        for dy in (1, 2, 3):
+            over_y(g, dy).wait_recv()
+        over_chip(g).start()
+
+    def take_chip(g):
+        over_chip(g).wait_recv()
+        assemble(g)
+
+    events = []
+    for g, (_, _, when) in enumerate(GROUPS):
+        events += [(when, take_plane, g), (when + Y_TIME, take_y, g), (when + Y_TIME + CHIP_TIME, take_chip, g)]
+    for _, take, g in sorted(events, key=lambda event: event[0]):
+        take(g)
 
     def drain(ref, sem):
         pltpu.make_async_remote_copy(
@@ -194,6 +214,15 @@
     for dy in (1, 2, 3):
         drain(held.at[core, 1 if dy == 2 else 0], y_send.at[dy - 1])
     drain(held.at[core, pl.ds(1, 4)], core_send)
+
+
+def write(*refs):
+    count = (len(refs) - 1) // 2
+    copies = [pltpu.make_async_copy(refs[i], refs[count + i], refs[-1].at[i]) for i in range(count)]
+    for copy in copies:
+        copy.start()
+    for copy in copies:
+        copy.wait()
 
 
 def per_device(master, grad, first_moment, second_moment, matching):
@@ -202,12 +231,13 @@
     cols = width // count
     total = 2 * count * 2 * rows
     hbm = pl.BlockSpec(memory_space=pltpu.HBM)
+    pin = functools.partial(pltpu.with_memory_space_constraint, memory_space=pltpu.HBM)
     vmem = pl.BlockSpec(memory_space=pltpu.VMEM)
     dma = pltpu.SemaphoreType.DMA
-    new_master, new_first, new_second, rollout = pl.pallas_call(
+    results = pl.pallas_call(
         kernel,
         out_shape=[pltpu.VMEM((rows, width), jnp.float32)] * 3 + [pltpu.VMEM((total, cols), jnp.bfloat16)],
-        in_specs=[hbm] * 4 + [vmem],
+        in_specs=[hbm] * 5,
         out_specs=[vmem] * 4,
         scratch_shapes=[
             pltpu.VMEM((rows, width), jnp.float32),
@@ -216,20 +246,29 @@
             pltpu.VMEM((rows, width), jnp.float32),
             pltpu.VMEM((count, 2 * rows, cols // 2), jnp.bfloat16),
             pltpu.VMEM((1, count), jnp.int32),
+            pltpu.VMEM((1, count), jnp.int32),
             pltpu.SMEM((1, count), jnp.int32),
             pltpu.VMEM((STEPS, 2, 2 * rows, cols // 2), jnp.bfloat16),
             pltpu.VMEM((2, 5, STEPS, 2 * rows, cols // 2), jnp.bfloat16),
             dma((4, CHUNKS)),
             dma,
             dma,
-            dma((GROUPS,)),
+            dma((len(GROUPS),)),
             dma((3,)),
-            dma((3, GROUPS)),
+            dma((3, len(GROUPS))),
             dma,
-            dma((GROUPS,)),
+            dma((len(GROUPS),)),
         ],
-        compiler_params=pltpu.CompilerParams(collective_id=0, has_side_effects=True, vmem_limit_bytes=30 << 20),
-    )(master, grad, first_moment, second_moment, matching.reshape(1, count))
+        compiler_params=pltpu.CompilerParams(collective_id=0, has_side_effects=True, vmem_limit_bytes=20 << 20),
+    )(*map(pin, (master, grad, first_moment, second_moment, matching.reshape(1, count))))
+    new_master, new_first, new_second, rollout = pl.pallas_call(
+        write,
+        out_shape=[jax.ShapeDtypeStruct(r.shape, r.dtype) for r in results],
+        in_specs=[vmem] * 4,
+        out_specs=[hbm] * 4,
+        scratch_shapes=[dma((4,))],
+        compiler_params=pltpu.CompilerParams(vmem_limit_bytes=4 << 20),
+    )(*(pltpu.with_memory_space_constraint(r, pltpu.VMEM) for r in results))
     return new_master, new_first, new_second, rollout.reshape(1, total, cols)
 
 

time: 53.8 us -> 47.8 us (0.89)
  local copies, waits for them, and re-layouts: 11.1 us -> 0 us
  Pallas kernels: 41.9 us -> 47 us
    unnamed x14 -> x0, local copies, waits for them, and re-layouts: 11.1 us -> none
    pallas_call x0 -> x1, Pallas kernels: none -> 3.26 us  [per_device(): pl.pallas_call(write, out_shape=[jax.ShapeDtypeStruct(r.shape, r.dtype) f...]
    pallas_call x1, Pallas kernels: 41.9 us -> 43.8 us  [per_device(): pl.pallas_call(kernel, out_shape=[pltpu.VMEM((rows, width), jnp.float32)]...]
where the time goes in v2:
time: 47.8 us; the launch traced here: 47.7 us
  Pallas kernels  47 us (98%)
  between operations  0.64 us (1%)
    pallas_call x1, Pallas kernels, per_device(): pl.pallas_call(kernel, out_shape=[pltpu.VMEM((rows, width), jnp.float32)]...  43.8 us
    pallas_call x1, Pallas kernels, per_device(): pl.pallas_call(write, out_shape=[jax.ShapeDtypeStruct(r.shape, r.dtype) f...  3.26 us

profile of v2, /device:TPU:1, one launch (start us, length us, event | category | flops | bytes accessed | tf_op | source)
XLA Modules:
  0.0 47.7 jit_solution(1674719597599860160)
XLA Ops:
  0.6 43.8 %shard_map.84 = (f32[24,16384]{1,0:T(8,128)S(1)}, f32[24,16384]{1,0:T(8,128)S(1)}, f32[24,16384]{1,0:T(8,128)S(1)}, bf16[6144,256]{1,0:T(8,128)(2,1)S(1)}) custom-call(f32[24,16384]{1,0:T(8,128)} %master_hbm.1, bf16[24,16384]{1,0:T(8,128)(2,1)} %grad_hbm.1, f32[24,16384]{1,0:T(8,128)} %first_hbm.1, f32[24,16384]{1,0:T(8,128)} %second_hbm.1, s32[1,64]{1,0:T(1,128)} %bitcast.2), custom_call_target="tpu_custom_call" | custom-call | tf_op jit(solution)/shard_map/pallas_call | solution.py:237
  44.4 3.3 %shard_map.85 = (f32[24,16384]{1,0:T(8,128)}, f32[24,16384]{1,0:T(8,128)}, f32[24,16384]{1,0:T(8,128)}, bf16[6144,256]{1,0:T(8,128)(2,1)}) custom-call(f32[24,16384]{1,0:T(8,128)S(1)} %get-tuple-element.12.refs_0_, f32[24,16384]{1,0:T(8,128)S(1)} %get-tuple-element.13.refs_1_, f32[24,16384]{1,0:T(8,128)S(1)} %get-tuple-element.14.refs_2_, ...), custom_call_target="tpu_custom_call" | custom-call | tf_op jit(solution)/shard_map/pallas_call | solution.py:264

commit v3 on v2

--- a/solution.py
+++ b/solution.py
@@ -18,12 +18,12 @@
 
 NX, NY, NZ = 4, 4, 8
 STEPS = NX * NZ
-GROUPS = (
-    (0, 4, 3.0), (4, 4, 6.0), (8, 4, 6.2), (12, 4, 10.0), (16, 4, 10.2),
-    (20, 2, 12.5), (24, 2, 12.7), (22, 2, 15.0), (26, 2, 15.2),
-    (28, 1, 15.6), (29, 1, 17.0), (30, 1, 18.5), (31, 1, 19.5),
+GROUPS = tuple((NX * j, NX) for j in range(NZ))
+ORDER = (
+    (3.0, 0, None), (6.0, 1, (True, 1)), (6.5, 2, None), (9.0, 3, (True, 2)), (10.0, 4, None), (11.5, 1, (False, 1)),
+    (13.0, 5, (True, 3)), (14.0, 6, None), (15.0, 3, (False, 2)), (17.0, 5, (False, 3)), (18.0, 7, None),
 )
-Y_TIME, CHIP_TIME = 3.5, 1.5
+Y_TIME, CHIP_TIME = 6.0, 4.0
 CHUNKS = 8
 
 
@@ -55,7 +55,7 @@
     master_hbm, grad_hbm, first_hbm, second_hbm, matching_hbm,
     new_master, new_first, new_second, rollout,
     master, grad, first, second, weights, matching, row, ranks, packed, held,
-    in_sem, rank_sem, plane_send, plane_recv, y_send, y_recv, core_send, core_recv,
+    in_sem, rank_sem, plane_send, plane_recv, y_send, y_recv, core_send, core_recv, down, up,
 ):
     rows, width = master.shape
     count = matching_hbm.shape[1]
@@ -80,15 +80,32 @@
 
     barrier = pltpu.get_barrier_semaphore()
 
-    def greet(k, carry):
-        dx, dz = offset(k)
-        pl.semaphore_signal(barrier, inc=1, device_id=device(x + dx, y, z + dz, core), device_id_type=MESH)
-        return carry
-
-    lax.fori_loop(1, STEPS, greet, 0)
-    for dy in (1, 2, 3):
-        pl.semaphore_signal(barrier, inc=1, device_id=device(x, y + dy, z, core), device_id_type=MESH)
-    pl.semaphore_signal(barrier, inc=1, device_id=other, device_id_type=MESH)
+    def greet(dx, dy, dz, dc):
+        pl.semaphore_signal(barrier, inc=1, device_id=device(x + dx, y + dy, z + dz, core + dc), device_id_type=MESH)
+
+    for n in (1, 2, 3):
+        greet(n, 0, 0, 0)
+        greet(0, n, 0, 0)
+    greet(0, 0, 0, 1)
+    greet(0, 0, -1, 0)
+
+    def tell(sem, j, dz):
+        pl.semaphore_signal(sem.at[j], inc=1, device_id=device(x, y, z + dz, core), device_id_type=MESH)
+
+    def enter():
+        pl.semaphore_wait(barrier, 8)
+        tell(down, 0, 1)
+
+    def hear_down(j):
+        pl.semaphore_wait(down.at[j - 1], 1)
+        tell(up, j - 1, -j)
+        if j < 3:
+            tell(down, j, 1)
+        elif j == 3:
+            pl.when((z >= 3) & (z < NZ - 1))(lambda: tell(down, 3, 1))
+
+    def hear_up(j):
+        pl.semaphore_wait(up.at[j - 1], 1)
 
     matching_load.wait()
     lane = lax.broadcasted_iota(jnp.int32, (count, count), 1)
@@ -114,6 +131,10 @@
             return carry
 
         lax.fori_loop(t * (count // CHUNKS), (t + 1) * (count // CHUNKS), block, 0)
+        if t == 3:
+            enter()
+        elif t > 3:
+            pl.when(z >= t - 3)(functools.partial(hear_down, t - 3))
 
     def piece(dx, dz, parity):
         host = ((z + NZ + dz) % NZ) * (2 * NX) + ((y + parity) % 2) * NX + (x + dx) % NX
@@ -121,7 +142,6 @@
 
     held[core, 0, 0] = piece(0, 0, 1)
     held[core, 1, 0] = piece(0, 0, 0)
-    pl.semaphore_wait(barrier, STEPS - 1 + 3 + 1)
 
     def sender(g):
         def send(k, carry):
@@ -140,11 +160,36 @@
 
         return send
 
-    for g, (low, size, _) in sorted(enumerate(GROUPS), key=lambda item: item[1][0]):
+    def send_group(g):
+        low, size = GROUPS[g]
         lax.fori_loop(max(low, 1), low + size, sender(g), 0)
 
+    def send_up(j):
+        hear_up(j)
+        send_group(2 * j - 1)
+
+    def send_down(j):
+        send_group(2 * j)
+
+    def send_down_late(j):
+        hear_down(j)
+        send_down(j)
+
+    send_group(0)
+    pl.when(z >= 1)(lambda: send_down(1))
+    send_up(1)
+    pl.when(z >= 2)(lambda: send_down(2))
+    send_up(2)
+    pl.when(z < 1)(lambda: send_down_late(1))
+    pl.when(z >= 3)(lambda: send_down(3))
+    pl.when(z < 2)(lambda: send_down_late(2))
+    send_up(3)
+    pl.when(z < 3)(lambda: send_down_late(3))
+    pl.when(z < 4)(lambda: hear_up(4))
+    send_group(7)
+
     def arrived(g):
-        low, size, _ = GROUPS[g]
+        low, size = GROUPS[g]
         low, size = max(low, 1), low + size - max(low, 1)
         where = held.at[core, pl.ds(0, 2), pl.ds(low, size)]
         return pltpu.make_async_remote_copy(
@@ -152,7 +197,7 @@
         )
 
     def over_y(g, dy):
-        here = pl.ds(*GROUPS[g][:2])
+        here = pl.ds(*GROUPS[g])
         return pltpu.make_async_remote_copy(
             src_ref=held.at[core, 1 if dy == 2 else 0, here],
             dst_ref=held.at[core, 1 + dy, here],
@@ -163,13 +208,13 @@
         )
 
     def over_chip(g):
-        where = held.at[core, pl.ds(1, 4), pl.ds(*GROUPS[g][:2])]
+        where = held.at[core, pl.ds(1, 4), pl.ds(*GROUPS[g])]
         return pltpu.make_async_remote_copy(
             src_ref=where, dst_ref=where, send_sem=core_send, recv_sem=core_recv.at[g], device_id=other, device_id_type=MESH
         )
 
     def assemble(g):
-        low, size, _ = GROUPS[g]
+        low, size = GROUPS[g]
 
         def block(n, carry):
             i, k = n // size, low + n % size
@@ -200,10 +245,13 @@
         assemble(g)
 
     events = []
-    for g, (_, _, when) in enumerate(GROUPS):
-        events += [(when, take_plane, g), (when + Y_TIME, take_y, g), (when + Y_TIME + CHIP_TIME, take_chip, g)]
-    for _, take, g in sorted(events, key=lambda event: event[0]):
-        take(g)
+    for when, g, only in ORDER:
+        events += [(when, take_plane, g, only), (when + Y_TIME, take_y, g, only), (when + Y_TIME + CHIP_TIME, take_chip, g, only)]
+    for _, take, g, only in sorted(events, key=lambda event: event[0]):
+        if only is None:
+            take(g)
+        else:
+            pl.when(z >= only[1] if only[0] else z < only[1])(functools.partial(take, g))
 
     def drain(ref, sem):
         pltpu.make_async_remote_copy(
@@ -258,6 +306,8 @@
             dma((3, len(GROUPS))),
             dma,
             dma((len(GROUPS),)),
+            pltpu.SemaphoreType.REGULAR((4,)),
+            pltpu.SemaphoreType.REGULAR((4,)),
         ],
         compiler_params=pltpu.CompilerParams(collective_id=0, has_side_effects=True, vmem_limit_bytes=20 << 20),
     )(*map(pin, (master, grad, first_moment, second_moment, matching.reshape(1, count))))

time: 47.8 us -> 45.2 us (0.946)
  the two profiles are of different devices: /device:TPU:1 before, /device:TPU:65 now
where the time goes in v3:
time: 45.2 us; the launch traced here: 44.5 us
  Pallas kernels  43.8 us (97%)
  between operations  0.64 us (1%)
    pallas_call x1, Pallas kernels, per_device(): pl.pallas_call(kernel, out_shape=[pltpu.VMEM((rows, width), jnp.float32)]...  40.6 us
    pallas_call x1, Pallas kernels, per_device(): pl.pallas_call(write, out_shape=[jax.ShapeDtypeStruct(r.shape, r.dtype) f...  3.26 us

profile of v3, /device:TPU:65, one launch (start us, length us, event | category | flops | bytes accessed | tf_op | source)
XLA Modules:
  0.0 44.5 jit_solution(5583043200480060920)
XLA Ops:
  0.6 40.6 %shard_map.84 = (f32[24,16384]{1,0:T(8,128)S(1)}, f32[24,16384]{1,0:T(8,128)S(1)}, f32[24,16384]{1,0:T(8,128)S(1)}, bf16[6144,256]{1,0:T(8,128)(2,1)S(1)}) custom-call(f32[24,16384]{1,0:T(8,128)} %master_hbm.1, bf16[24,16384]{1,0:T(8,128)(2,1)} %grad_hbm.1, f32[24,16384]{1,0:T(8,128)} %first_hbm.1, f32[24,16384]{1,0:T(8,128)} %second_hbm.1, s32[1,64]{1,0:T(1,128)} %bitcast.2), custom_call_target="tpu_custom_call" | custom-call | tf_op jit(solution)/shard_map/pallas_call | solution.py:285
  41.2 3.3 %shard_map.85 = (f32[24,16384]{1,0:T(8,128)}, f32[24,16384]{1,0:T(8,128)}, f32[24,16384]{1,0:T(8,128)}, bf16[6144,256]{1,0:T(8,128)(2,1)}) custom-call(f32[24,16384]{1,0:T(8,128)S(1)} %get-tuple-element.12.refs_0_, f32[24,16384]{1,0:T(8,128)S(1)} %get-tuple-element.13.refs_1_, f32[24,16384]{1,0:T(8,128)S(1)} %get-tuple-element.14.refs_2_, ...), custom_call_target="tpu_custom_call" | custom-call | tf_op jit(solution)/shard_map/pallas_call | solution.py:314

commit v4 on v2

v4 whole, which is shorter than its diff:
```python
import functools

import jax
import jax.numpy as jnp
from jax import lax
from jax.experimental import pallas as pl
from jax.experimental.pallas import tpu as pltpu
from jax.sharding import PartitionSpec as P

MESH = pl.DeviceIdType.MESH
beta_one = 0.9
beta_two = 0.95
learn_rate = 0.05
decay_rate = 0.1
epsilon = 1e-08
bias_one = 1.0 - 0.9**10
bias_two = 1.0 - 0.95**10

NX, NY, NZ = 4, 4, 8
STEPS = NX * NZ
CHUNKS = 4
UNROLL = 8

GROUPS = tuple((NX * (j + 1) + (0, 1, 3)[n], (1, 2, 1)[n]) for j in range(NZ - 1) for n in range(3))
NEAR = len(GROUPS)
TIMES = (
    (1, (4.0, 5.0, 5.8), lambda z: z >= 1), (2, (4.1, 5.1, 5.9), None), (3, (6.5, 7.5, 8.2), lambda z: z >= 2), (4, (7.0, 8.0, 9.0), None),
    (1, (9.5, 10.0, 10.5), lambda z: z < 1), (5, (10.5, 11.5, 12.5), lambda z: z >= 3), (6, (11.0, 12.0, 13.0), None),
    (3, (13.0, 13.5, 14.0), lambda z: z < 2), (5, (15.0, 15.5, 16.0), lambda z: z < 3), (7, (15.1, 16.1, 17.0), None),
)
SENDS = (
    (0.05, 2, lambda z: z >= 1, True, True), (0.2, 4, lambda z: z >= 2, True, True), (0.3, 6, lambda z: z >= 3, True, True),
    (1.2, 1, None, True, True), (1.3, 7, lambda z: z >= 4, True, False), (1.8, 3, None, True, True), (3.2, 2, lambda z: z < 1, True, True),
    (3.3, 5, None, True, True), (3.4, 4, lambda z: z < 2, True, True), (4.4, 6, lambda z: z < 3, True, True),
    (4.5, 7, lambda z: z < 4, True, False), (4.6, 7, None, False, True),
)
Y_TIME = 6.0

def place():
    pool, fsdp, core = lax.axis_index("pool"), lax.axis_index("fsdp"), lax.axis_index("rep")
    return fsdp % NX, pool * 2 + (fsdp // NX) % 2, fsdp // (2 * NX), core


def device(x, y, z, core):
    x, y, z, core = (x + NX) % NX, (y + NY) % NY, (z + NZ) % NZ, core % 2
    return (y // 2, z * (2 * NX) + (y % 2) * NX + x, core)


def offset(k):
    i, j = k % NX, k // NX
    return i + (i // 2) * (1 - 2 * (i % 2)), ((j + 1) // 2) * (2 * (j % 2) - 1)


def adamw(master, grad, first, second):
    gradient = grad.astype(jnp.float32)
    new_first = beta_one * first + (1.0 - beta_one) * gradient
    new_second = beta_two * second + (1.0 - beta_two) * gradient * gradient
    scaled = new_second * (1.0 / bias_two)
    root = scaled * lax.rsqrt(scaled)
    step = new_first * (learn_rate / bias_one)
    new_master = master * (1.0 - learn_rate * decay_rate) - step / (root + epsilon)
    return new_master, new_first, new_second


def kernel(
    master_hbm, grad_hbm, first_hbm, second_hbm, matching_hbm,
    new_master, new_first, new_second, held,
    master, grad, first, second, weights, matching, row, ranks, packed,
    in_sem, rank_sem, plane_send, plane_recv, y_send, y_recv, core_send, core_recv, near_send, near_recv, down, up,
):
    rows, width = master.shape
    count = matching_hbm.shape[1]
    cols = width // count
    half = cols // 2
    x, y, z, core = place()
    other = device(x, y, z, core + 1)

    matching_load = pltpu.make_async_copy(matching_hbm, matching, rank_sem)
    matching_load.start()
    grad_load = pltpu.make_async_copy(grad_hbm, grad, in_sem.at[0, 0])
    grad_load.start()

    def load(t, i):
        where = pl.ds(t * (width // CHUNKS), width // CHUNKS)
        src, dst = ((master_hbm, master), (first_hbm, first), (second_hbm, second))[i]
        return pltpu.make_async_copy(src.at[:, where], dst.at[:, where], in_sem.at[1 + i, t])

    for t in range(CHUNKS):
        for i in range(3):
            load(t, i).start()

    barrier = pltpu.get_barrier_semaphore()

    def greet(dx, dy, dz, dc):
        pl.semaphore_signal(barrier, inc=1, device_id=device(x + dx, y + dy, z + dz, core + dc), device_id_type=MESH)

    def greet_near(n, carry):
        greet(n % NX, n // NX, 0, 0)
        return carry

    greet(0, 0, 0, 1)
    greet(0, 0, -1, 0)
    lax.fori_loop(1, NX * NY, greet_near, 0)

    def tell(sem, j, dz):
        pl.semaphore_signal(sem.at[j], inc=1, device_id=device(x, y, z + dz, core), device_id_type=MESH)

    def enter():
        pl.semaphore_wait(barrier, 2 + NX * NY - 1)
        tell(down, 0, 1)

    def hear_down(j):
        pl.semaphore_wait(down.at[j - 1], 1)
        tell(up, j - 1, -j)
        if j < 3:
            tell(down, j, 1)
        elif j == 3:
            pl.when((z >= 3) & (z < NZ - 1))(lambda: tell(down, 3, 1))

    def hear_up(j):
        pl.semaphore_wait(up.at[j - 1], 1)

    to_scalar = pltpu.make_async_copy(row, ranks, rank_sem)

    def look_up():
        matching_load.wait()
        lane = lax.broadcasted_iota(jnp.int32, (count, count), 1)
        sub = lax.broadcasted_iota(jnp.int32, (count, count), 0)
        hit = jnp.where(matching[...] == sub, lane, 0)
        column = jnp.max(hit, axis=1, keepdims=True)
        row[...] = jnp.sum(jnp.where(lane == sub, column, 0), axis=0, keepdims=True)
        to_scalar.start()

    grad_load.wait()
    for t in range(CHUNKS):
        for i in range(3):
            load(t, i).wait()

        def blocks(n, carry):
            for u in range(UNROLL):
                where = pl.ds(pl.multiple_of((n * UNROLL + u) * cols, cols), cols)
                value, new_first[:, where], new_second[:, where] = adamw(
                    master[:, where], grad[:, where], first[:, where], second[:, where]
                )
                new_master[:, where] = value
                value = jnp.concatenate([value[:, :half], value[:, half:]], axis=0)
                weights[n * UNROLL + u] = value.astype(jnp.bfloat16)
            return carry

        per = count // CHUNKS // UNROLL
        lax.fori_loop(t * per, (t + 1) * per, blocks, 0)
        if t == 1:
            look_up()
        elif t == 3:
            enter()
    to_scalar.wait()

    across = [lax.rem(x + offset(i)[0], NX) for i in range(NX)]
    lows = (lax.rem(y + 1, 2) * NX, lax.rem(y, 2) * NX)
    near_hosts = [(across[i] + lows[0], across[i] + lows[1]) for i in range(NX)]

    def pack(j, carry):
        plane = lax.rem(z + NZ + offset(j * NX)[1], NZ) * (2 * NX)
        for i in range(NX):
            for own in (0, 1):
                packed[j * NX + i, own] = weights[ranks[0, plane + near_hosts[i][own]]]
        return carry

    lax.fori_loop(0, NZ, pack, 0)
    held[core, 1, 0] = packed[0, 1]

    for k in range(NX):
        for dy in (2, 1, 3, 0) if k else (2, 1, 3):
            pltpu.make_async_remote_copy(
                src_ref=packed.at[k, (dy + 1) % 2],
                dst_ref=held.at[core, 1 + dy, k],
                send_sem=y_send.at[dy - 1] if dy else near_send,
                recv_sem=y_recv.at[dy - 1, NEAR] if dy else near_recv,
                device_id=device(x + offset(k)[0], y + dy, z, core),
                device_id_type=MESH,
            ).start()

    def send_plane(j):
        plane = lax.rem(z + NZ + offset(j * NX)[1], NZ) * (2 * NX)
        for i in range(NX):
            k = j * NX + i
            pltpu.make_async_remote_copy(
                src_ref=packed.at[k],
                dst_ref=held.at[core, pl.ds(0, 2), k],
                send_sem=plane_send,
                recv_sem=plane_recv.at[(j - 1) * 3 + (0, 1, 1, 2)[i]],
                device_id=(y // 2, plane + near_hosts[i][1], core),
                device_id_type=MESH,
            ).start()

    def hear(j, late):
        if j == 7 and late:
            hear_up(4)
        elif j % 2 and j < 7:
            hear_up((j + 1) // 2)
        else:
            hear_down((j + 1) // 2)

    lines = {dy: device(x, y + dy, z, core) for dy in (1, 2, 3)}

    def arrived(g):
        where = held.at[core, pl.ds(0, 2), pl.ds(*GROUPS[g])]
        return pltpu.make_async_remote_copy(
            src_ref=where, dst_ref=where, send_sem=plane_send, recv_sem=plane_recv.at[g], device_id=other, device_id_type=MESH
        )

    def near(sem):
        where = held.at[core, 1, pl.ds(1, NX - 1)]
        return pltpu.make_async_remote_copy(
            src_ref=where, dst_ref=where, send_sem=near_send, recv_sem=sem, device_id=other, device_id_type=MESH
        )

    def over_y(g, dy):
        here = pl.ds(0, NX) if g == NEAR else pl.ds(*GROUPS[g])
        return pltpu.make_async_remote_copy(
            src_ref=held.at[core, 1 if dy == 2 else 0, here],
            dst_ref=held.at[core, 1 + dy, here],
            send_sem=y_send.at[dy - 1],
            recv_sem=y_recv.at[dy - 1, g],
            device_id=lines[dy],
            device_id_type=MESH,
        )

    def over_chip(n):
        where = held.at[core, pl.ds(1, 4), pl.ds(n * NX, NX)]
        return pltpu.make_async_remote_copy(
            src_ref=where, dst_ref=where, send_sem=core_send, recv_sem=core_recv.at[n], device_id=other, device_id_type=MESH
        )

    def take_plane(g):
        arrived(g).wait_recv()
        for dy in (1, 2, 3):
            over_y(g, dy).start()

    def take_y(g):
        for dy in (1, 2, 3):
            over_y(g, dy).wait_recv()
        if g == NEAR:
            near(near_recv).wait_recv()
            over_chip(0).start()
        elif g % 3 == 2:
            over_chip(g // 3 + 1).start()

    events = [(5.0, None, functools.partial(take_y, NEAR))]
    for when, j, only, listen, go in SENDS:
        if listen:
            events.append((when, only, functools.partial(hear, j, when > 4)))
        if go:
            events.append((when + 0.001, only, functools.partial(send_plane, j)))
    for j, times, only in TIMES:
        for n, when in enumerate(times):
            g = (j - 1) * 3 + n
            events.append((when, only, functools.partial(take_plane, g)))
            events.append((when + Y_TIME, only, functools.partial(take_y, g)))
    for _, only, take in sorted(events, key=lambda event: event[0]):
        if only is None:
            take()
        else:
            pl.when(only(z))(take)

    for n in range(NZ):
        over_chip(n).wait_recv()

    def drain(ref, sem):
        pltpu.make_async_remote_copy(
            src_ref=ref, dst_ref=ref, send_sem=sem, recv_sem=plane_recv.at[0], device_id=other, device_id_type=MESH
        ).wait_send()

    near(near_recv).wait_send()
    drain(packed.at[pl.ds(NX, STEPS - NX)], plane_send)
    for dy in (1, 2, 3):
        drain(held.at[core, 1 if dy == 2 else 0], y_send.at[dy - 1])
    drain(held.at[core, pl.ds(1, 4)], core_send)


def write(new_master, new_first, new_second, held, out_master, out_first, out_second, out_rollout, rollout, whole_sem, part_sem):
    x, y, z, _ = place()
    rows = new_master.shape[0]
    count = NX * 2 * NZ
    wholes = [
        pltpu.make_async_copy(src, dst, whole_sem.at[i])
        for i, (src, dst) in enumerate(((new_master, out_master), (new_first, out_first), (new_second, out_second)))
    ]

    def block(i, k):
        dx, dz = offset(k)
        pool, fsdp, _ = device(x + NX - dx, y + NY - i, z + NZ - dz, 0)
        start = pl.multiple_of((pool * count + fsdp) * (2 * rows), 2 * rows)
        parts = []
        for c in (0, 1):
            value = held[c, 1 + i, k].astype(jnp.float32)
            parts.append(jnp.concatenate([value[:rows], value[rows:]], axis=1))
        rollout[pl.ds(start, 2 * rows), :] = jnp.concatenate(parts, axis=0).astype(jnp.bfloat16)

    def part(j, pool):
        _, dz = offset(j * NX)
        size = NX * 2 * 2 * rows
        where = pl.ds(pl.multiple_of((pool * NZ + (z + NZ - dz) % NZ) * size, size), size)
        return pltpu.make_async_copy(rollout.at[where], out_rollout.at[where], part_sem.at[j, pool])

    for j in range(NZ):

        def blocks(n, carry):
            for i in range(NY):
                block(i, j * NX + n)
            return carry

        lax.fori_loop(0, NX, blocks, 0)
        for pool in (0, 1):
            part(j, pool).start()
        if j < len(wholes):
            wholes[j].start()
    for copy in wholes:
        copy.wait()
    for j in range(NZ):
        for pool in (0, 1):
            part(j, pool).wait()


def per_device(master, grad, first_moment, second_moment, matching):
    rows, width = master.shape
    count = matching.shape[0]
    cols = width // count
    total = 2 * count * 2 * rows
    hbm = pl.BlockSpec(memory_space=pltpu.HBM)
    pin = functools.partial(pltpu.with_memory_space_constraint, memory_space=pltpu.HBM)
    vmem = pl.BlockSpec(memory_space=pltpu.VMEM)
    dma = pltpu.SemaphoreType.DMA
    results = pl.pallas_call(
        kernel,
        out_shape=[pltpu.VMEM((rows, width), jnp.float32)] * 3 + [pltpu.VMEM((2, 1 + NY, STEPS, 2 * rows, cols // 2), jnp.bfloat16)],
        in_specs=[hbm] * 5,
        out_specs=[vmem] * 4,
        scratch_shapes=[
            pltpu.VMEM((rows, width), jnp.float32),
            pltpu.VMEM((rows, width), jnp.bfloat16),
            pltpu.VMEM((rows, width), jnp.float32),
            pltpu.VMEM((rows, width), jnp.float32),
            pltpu.VMEM((count, 2 * rows, cols // 2), jnp.bfloat16),
            pltpu.VMEM((1, count), jnp.int32),
            pltpu.VMEM((1, count), jnp.int32),
            pltpu.SMEM((1, count), jnp.int32),
            pltpu.VMEM((STEPS, 2, 2 * rows, cols // 2), jnp.bfloat16),
            dma((4, CHUNKS)),
            dma,
            dma,
            dma((len(GROUPS),)),
            dma((3,)),
            dma((3, len(GROUPS) + 1)),
            dma,
            dma((NZ,)),
            dma,
            dma,
            pltpu.SemaphoreType.REGULAR((4,)),
            pltpu.SemaphoreType.REGULAR((4,)),
        ],
        compiler_params=pltpu.CompilerParams(collective_id=0, has_side_effects=True, vmem_limit_bytes=20 << 20),
    )(*map(pin, (master, grad, first_moment, second_moment, matching.reshape(1, count))))
    new_master, new_first, new_second, rollout = pl.pallas_call(
        write,
        out_shape=[jax.ShapeDtypeStruct((rows, width), jnp.float32)] * 3 + [jax.ShapeDtypeStruct((total, cols), jnp.bfloat16)],
        in_specs=[vmem] * 4,
        out_specs=[hbm] * 4,
        scratch_shapes=[pltpu.VMEM((total, cols), jnp.bfloat16), dma((3,)), dma((NZ, 2))],
        compiler_params=pltpu.CompilerParams(vmem_limit_bytes=8 << 20),
    )(*(pltpu.with_memory_space_constraint(r, pltpu.VMEM) for r in results))
    return new_master, new_first, new_second, rollout.reshape(1, total, cols)


def solution(mesh):
    rows = P(("pool", "fsdp", "rep"), None)
    return jax.shard_map(
        per_device,
        mesh=mesh,
        in_specs=(rows, rows, rows, rows, P()),
        out_specs=(rows, rows, rows, P("fsdp", None, None)),
        check_vma=False,
    )
```

time: 47.8 us -> 44 us (0.921)
  the two profiles are of different devices: /device:TPU:1 before, /device:TPU:65 now
where the time goes in v4:
time: 44 us; the launch traced here: 43.9 us
  Pallas kernels  43.3 us (98%)
  between operations  0.64 us (1%)
    pallas_call x1, Pallas kernels, per_device(): pl.pallas_call(kernel, out_shape=[pltpu.VMEM((rows, width), jnp.float32)]...  39.7 us
    pallas_call x1, Pallas kernels, per_device(): pl.pallas_call(write, out_shape=[jax.ShapeDtypeStruct((rows, width), jnp....  3.6 us

profile of v4, /device:TPU:65, one launch (start us, length us, event | category | flops | bytes accessed | tf_op | source)
XLA Modules:
  0.0 43.9 jit_solution(2915681449331670323)
XLA Ops:
  0.6 39.7 %shard_map.84 = (f32[24,16384]{1,0:T(8,128)S(1)}, f32[24,16384]{1,0:T(8,128)S(1)}, f32[24,16384]{1,0:T(8,128)S(1)}, bf16[2,5,32,48,128]{4,3,2,1,0:T(8,128)(2,1)S(1)}) custom-call(f32[24,16384]{1,0:T(8,128)} %master_hbm.1, bf16[24,16384]{1,0:T(8,128)(2,1)} %grad_hbm.1, f32[24,16384]{1,0:T(8,128)} %first_hbm.1, f32[24,16384]{1,0:T(8,128)} %second_hbm.1, ...), custom_call_target="tpu_custom_call" | custom-call | tf_op jit(solution)/shard_map/pallas_call | solution.py:334
  40.3 3.6 %shard_map.85 = (f32[24,16384]{1,0:T(8,128)}, f32[24,16384]{1,0:T(8,128)}, f32[24,16384]{1,0:T(8,128)}, bf16[6144,256]{1,0:T(8,128)(2,1)}) custom-call(f32[24,16384]{1,0:T(8,128)S(1)} %get-tuple-element.12.new_master, f32[24,16384]{1,0:T(8,128)S(1)} %get-tuple-element.13.new_first, f32[24,16384]{1,0:T(8,128)S(1)} %get-tuple-element.14.new_second, ...), custom_call_target="tpu_custom_call" | custom-call | tf_op jit(solution)/shard_map/pallas_call | solution.py:364

commit v5 on v4

--- a/solution.py
+++ b/solution.py
@@ -303,6 +303,8 @@
         where = pl.ds(pl.multiple_of((pool * NZ + (z + NZ - dz) % NZ) * size, size), size)
         return pltpu.make_async_copy(rollout.at[where], out_rollout.at[where], part_sem.at[j, pool])
 
+    for copy in wholes:
+        copy.start()
     for j in range(NZ):
 
         def blocks(n, carry):
@@ -313,8 +315,6 @@
         lax.fori_loop(0, NX, blocks, 0)
         for pool in (0, 1):
             part(j, pool).start()
-        if j < len(wholes):
-            wholes[j].start()
     for copy in wholes:
         copy.wait()
     for j in range(NZ):

time: 44 us -> 43.7 us (level)
  no operation moved by 1% of the time
where the time goes in v5:
time: 43.7 us; the launch traced here: 43.6 us
  Pallas kernels  43 us (98%)
  between operations  0.64 us (1%)
    pallas_call x1, Pallas kernels, per_device(): pl.pallas_call(kernel, out_shape=[pltpu.VMEM((rows, width), jnp.float32)]...  39.7 us
    pallas_call x1, Pallas kernels, per_device(): pl.pallas_call(write, out_shape=[jax.ShapeDtypeStruct((rows, width), jnp....  3.29 us

profile of v5, /device:TPU:65, one launch (start us, length us, event | category | flops | bytes accessed | tf_op | source)
XLA Modules:
  0.0 43.6 jit_solution(14408456916618852628)
XLA Ops:
  0.6 39.7 %shard_map.84 = (f32[24,16384]{1,0:T(8,128)S(1)}, f32[24,16384]{1,0:T(8,128)S(1)}, f32[24,16384]{1,0:T(8,128)S(1)}, bf16[2,5,32,48,128]{4,3,2,1,0:T(8,128)(2,1)S(1)}) custom-call(f32[24,16384]{1,0:T(8,128)} %master_hbm.1, bf16[24,16384]{1,0:T(8,128)(2,1)} %grad_hbm.1, f32[24,16384]{1,0:T(8,128)} %first_hbm.1, f32[24,16384]{1,0:T(8,128)} %second_hbm.1, ...), custom_call_target="tpu_custom_call" | custom-call | tf_op jit(solution)/shard_map/pallas_call | solution.py:334
  40.3 3.3 %shard_map.85 = (f32[24,16384]{1,0:T(8,128)}, f32[24,16384]{1,0:T(8,128)}, f32[24,16384]{1,0:T(8,128)}, bf16[6144,256]{1,0:T(8,128)(2,1)}) custom-call(f32[24,16384]{1,0:T(8,128)S(1)} %get-tuple-element.12.new_master, f32[24,16384]{1,0:T(8,128)S(1)} %get-tuple-element.13.new_first, f32[24,16384]{1,0:T(8,128)S(1)} %get-tuple-element.14.new_second, ...), custom_call_target="tpu_custom_call" | custom-call | tf_op jit(solution)/shard_map/pallas_call | solution.py:364
